TPU v7x, 256 devices: a whole 4x4x8 slice. The times are simulated.
256 devices in a mesh: con: 16 (over z_hi, x, core), res: 16 (over y, z_lo).
Axes of the slice: x: 4, y: 4, z: 8 (z_hi: 2, z_lo: 4; z = z_hi * 4 + z_lo), core: 2. Of those that a mesh axis runs over, the one named last changes fastest.
Arguments:
- integrals: float32 [24576, 24576], P('res', 'con'), as said below
- tile_mask: int32 [96, 96], P('res', 'con'), may hold values from 0 to 1, as said below
- amplitudes: float32 [24576, 384], P(('con', 'res')), may hold values from -4 to 4
- other_first: float32 [24576, 384], P(('res', 'con')), may hold values from -6 to 6
- other_second: float32 [24576, 384], P(('con', 'res')), may hold values from -6 to 6
- vir_index: int32 [2, 24576], replicated, may hold values from 0 to 1599
- occ_index: int32 [2, 384], replicated, may hold values from 0 to 31, as said below
- partner: int32 [384], replicated, may hold values from 0 to 383, as said below
- eps_vir: float32 [1600], replicated, may hold values from 0.2 to 3
- eps_occ: float32 [32], replicated, may hold values from -2 to -0.2
Outputs:
- first_update: float32 [24576, 384], P(('res', 'con'))
- second_update: float32 [24576, 384], P(('con', 'res'))
Inputs may be any that keep to these rules, and one draw needn't show every extreme that they name: integrals is symmetric: integrals[p, s] == integrals[s, p]. tile_mask is symmetric and its diagonal is 1. partner is a permutation that is its own inverse with no fixed point. The two orbitals of an occupied pair differ, and occ_index[0, partner[q]] == occ_index[1, q].
All inputs are finite; a program needn't handle non-finite values.
Results may differ from a plain program's by a relative error of at most 0.000065.
Values sent between devices are 32-bit elements; how exact they have to be, the bound alone decides.
A program may use at most 128 MiB of HBM per device.

v0:
```python
import jax
import jax.numpy as jnp
from jax import lax
from jax.sharding import PartitionSpec as P

W = 256
exact = lax.Precision.HIGHEST
three = lax.Precision.HIGH


def pick(index, table):
    places = lax.broadcasted_iota(jnp.int32, (index.shape[0], table.shape[0]), 1)
    hits = (index[:, None] == places).astype(jnp.float32)
    return jnp.sum(hits * table[None, :], axis=1)


def pair_energy(pair_index, table):
    return pick(pair_index[0], table) + pick(pair_index[1], table)


def pair_map(partner):
    cols = partner.shape[0]
    here = lax.broadcasted_iota(jnp.int32, (cols,), 0)
    first = here < partner
    key = jnp.minimum(here, partner)
    couple = jnp.sum((first[None, :] & (here[None, :] < key[:, None])).astype(jnp.int32), axis=1)
    hit = couple[:, None] == lax.broadcasted_iota(jnp.int32, (cols, cols // 2), 1)
    return jnp.where(hit, jnp.where(first, 1.0, -1.0)[:, None], 0.0)


def per_device(
    integrals,
    tile_mask,
    amplitudes,
    other_first,
    other_second,
    vir_index,
    occ_index,
    partner,
    eps_vir,
    eps_occ,
):
    row_count, col_count = integrals.shape
    tiles_down, tiles_across = tile_mask.shape
    weights = tile_mask.astype(jnp.float32)
    screened = (
        integrals.reshape(tiles_down, W, tiles_across, W) * weights[:, None, :, None]
    ).reshape(row_count, col_count)
    pairs = pair_map(partner)
    occ_energy = pair_energy(occ_index, eps_occ)
    occ_energy = jnp.sum(jnp.where(pairs > 0, occ_energy[:, None], 0.0), axis=0)
    n_con = lax.axis_size("con")
    n_res = lax.axis_size("res")
    con_at = lax.axis_index("con")
    res_at = lax.axis_index("res")
    fine_rows = amplitudes.shape[0]

    def differences(block):
        return jnp.dot(block, pairs, precision=exact, preferred_element_type=jnp.float32)

    def spread(half):
        return 0.5 * lax.dot_general(
            half,
            pairs,
            (((1,), (1,)), ((), ())),
            precision=exact,
            preferred_element_type=jnp.float32,
        )

    def denominator(offset):
        picked = lax.dynamic_slice_in_dim(vir_index, offset, fine_rows, 1)
        return pair_energy(picked, eps_vir)[:, None] - occ_energy[None, :]

    own = differences(amplitudes)
    partial_one = jnp.dot(
        screened,
        lax.all_gather(own, "res", axis=0, tiled=True),
        precision=three,
        preferred_element_type=jnp.float32,
    )
    ladder_one = lax.psum_scatter(partial_one, "con", scatter_dimension=0, tiled=True)
    first = (differences(other_first) + ladder_one) / denominator(
        (res_at * n_con + con_at) * fine_rows
    )
    partial_two = lax.dot_general(
        screened,
        lax.all_gather(first, "con", axis=0, tiled=True),
        (((0,), (0,)), ((), ())),
        precision=three,
        preferred_element_type=jnp.float32,
    )
    ladder_two = lax.psum_scatter(partial_two, "res", scatter_dimension=0, tiled=True)
    second = (differences(other_second) + ladder_two) / denominator(
        (con_at * n_res + res_at) * fine_rows
    )
    return (spread(first), spread(second))


def solution(mesh):
    return jax.shard_map(
        per_device,
        mesh=mesh,
        in_specs=(
            P("res", "con"),
            P("res", "con"),
            P(("con", "res"), None),
            P(("res", "con"), None),
            P(("con", "res"), None),
            P(),
            P(),
            P(),
            P(),
            P(),
        ),
        out_specs=(P(("res", "con"), None), P(("con", "res"), None)),
        check_vma=False,
    )
```

profile of v0, /device:TPU:4, one launch (start us, length us, event | category | flops | bytes accessed | tf_op | source)
XLA Modules:
  0.0 355.9 jit_solution(8949137891145068009)
XLA Ops:
  7.2 0.7 broadcast_select_fusion
  7.9 0.7 iota_minimum_fusion
  8.9 0.4 convolution_bitcast_fusion.1
  9.3 0.7 copy.18
  10.1 0.7 convert_element_type.5
  10.8 0.9 mul.69
  11.7 8.4 %copy.28 = f32[192,8,6,256]{3,1,2,0:T(8,128)} copy(f32[192,8,6,256]{3,2,1,0:T(8,128)S(1)} %bitcast.36) | data formatting | bytes 18874368
  20.0 12.2 %mul.71 = f32[1536,1536]{1,0:T(8,128)} multiply(f32[1536,1536]{1,0:T(8,128)} %param.10, f32[1536,1536]{1,0:T(8,128)} %bitcast.37) | non-fusion elementwise | flops 2359296 | bytes 28311552 | tf_op jit(solution)/shard_map/mul | solution.py:47
  32.3 65.8 %all-gather.3.cloned.1.call-done = f32[1536,192]{1,0:T(8,128)} async-done(((f32[96,192]{1,0:T(8,128)}), f32[1536,192]{1,0:T(8,128)}) %all-gather.3.cloned.1.call-update) | async-done | bytes 1179664 | tf_op jit(solution)/shard_map/all_gather | solution.py:77
  98.1 9.3 %fusion.30 = f32[1536,192]{1,0:T(8,128)} fusion(f32[1536,1536]{1,0:T(8,128)} %mul.71, f32[1536,192]{1,0:T(8,128)} %all-gather.3.cloned.1.call-done), kind=kOutput, calls=%fused_computation.63 | convolution fusion | flops 2717908992 | bytes 11796480
  107.5 0.6 copy-done.2
  108.2 0.8 constant_dynamic-slice_fusion.1
  109.0 0.5 select_reduce_fusion
  109.6 78.8 %reduce-scatter.7.cloned.1.call-done = f32[96,192]{1,0:T(8,128)} async-done(((f32[1536,192]{1,0:T(8,128)}), f32[96,192]{1,0:T(8,128)}) %reduce-scatter.7.cloned.1.call-update) | async-done | bytes 73744
  188.4 1.0 copy.25
  189.4 0.4 fusion.3
  189.9 0.7 copy.20
  190.7 56.7 %all-gather.5.cloned.1.call-done = f32[1536,192]{1,0:T(8,128)} async-done(((f32[96,192]{1,0:T(8,128)}), f32[1536,192]{1,0:T(8,128)}) %all-gather.5.cloned.1.call-update) | async-done | bytes 1179664 | tf_op jit(solution)/shard_map/all_gather | solution.py:87
  247.4 12.8 %fusion.31 = f32[1536,192]{1,0:T(8,128)} fusion(f32[1536,1536]{1,0:T(8,128)} %mul.71, f32[1536,192]{1,0:T(8,128)} %all-gather.5.cloned.1.call-done), kind=kOutput, calls=%fused_computation.64 | convolution fusion | flops 2717908992 | bytes 11796480
  260.2 1.1 convolution_multiply_fusion.1
  261.3 85.5 %reduce-scatter.9.cloned.1.call-done = f32[96,192]{1,0:T(8,128)} async-done(((f32[1536,192]{1,0:T(8,128)}), f32[96,192]{1,0:T(8,128)}) %reduce-scatter.9.cloned.1.call-update) | async-done | bytes 73744
  346.8 1.0 copy.27
  347.8 0.4 fusion.1
  348.3 1.1 convolution_multiply_fusion
  (27 shorter events, 0.8 us)
Async XLA Ops:
  7.2 1.7 copy-start
  7.2 90.9 %all-gather.3.cloned.1.call-start = ((), (), s32[]{:S(2)}) async-start(), calls=%async_computation.2 | async-start | bytes 1671168 | tf_op jit(solution)/shard_map/all_gather | solution.py:77
  10.0 178.4 %reduce-scatter.7.cloned.1.call-start = ((), (), s32[]{:S(2)}) async-start(), calls=%async_computation.4 | async-start | bytes 1671168
  107.4 0.7 copy-start.2
  107.4 0.7 copy-start.3
  107.4 1.6 copy-start.1
  107.4 82.0 %copy-start.4 = (f32[96,384]{1,0:T(8,128)S(1)}, f32[96,384]{1,0:T(8,128)}, u32[]{:S(2)}) copy-start(f32[96,384]{1,0:T(8,128)} %param.13) | copy-start | bytes 442372
  107.4 139.9 %all-gather.5.cloned.1.call-start = ((), (), s32[]{:S(2)}) async-start(), calls=%async_computation.3 | async-start | bytes 1671168 | tf_op jit(solution)/shard_map/all_gather | solution.py:87
  190.6 156.2 %reduce-scatter.9.cloned.1.call-start = ((), (), s32[]{:S(2)}) async-start(), calls=%async_computation.5 | async-start | bytes 1671168
  260.2 87.6 %copy-start.5 = (f32[96,384]{1,0:T(8,128)S(1)}, f32[96,384]{1,0:T(8,128)}, u32[]{:S(2)}) copy-start(f32[96,384]{1,0:T(8,128)} %param.14) | copy-start | bytes 442372
Sparse Core Ops, SparseCore 0:
  10.4 87.6 all-gather.2
  107.5 80.8 reduce-scatter.6
  191.8 55.5 all-gather.4
  260.4 86.4 reduce-scatter.8
where the time goes:
time: 356 us
  waiting for transfers between devices  287 us (81%)
  matrix products  25.5 us (7%)
  other arithmetic  15.3 us (4%)
  local copies, waits for them, and re-layouts  14.1 us (4%)
  between operations  13.9 us (4%)
    unnamed x6, waiting for transfers between devices  164 us
    all_gather x1, waiting for transfers between devices, per_device(): lax.all_gather(own, 'res', axis=0, tiled=True)  65.8 us
    all_gather x1, waiting for transfers between devices, per_device(): lax.all_gather(first, 'con', axis=0, tiled=True)  56.7 us
    unnamed x2, matrix products  22.1 us
    mul x1, other arithmetic, per_device(): integrals.reshape(tiles_down, W, tiles_across, W)  12.2 us
    unnamed x15, local copies, waits for them, and re-layouts  10.9 us
  transfers between devices with their start and end apart: 4, of which 4 were waited for; matrix products, arithmetic and copies ran while one was open for 7% of the time, Pallas kernels for 0%

commit v1 on v0

--- a/solution.py
+++ b/solution.py
@@ -84,7 +84,9 @@
     )
     partial_two = lax.dot_general(
         screened,
-        lax.all_gather(first, "con", axis=0, tiled=True),
+        jnp.concatenate(
+            lax.all_to_all(jnp.stack([first] * lax.axis_size("con")), "con", 0, 0), axis=0
+        ),
         (((0,), (0,)), ((), ())),
         precision=three,
         preferred_element_type=jnp.float32,

time: 356 us -> 344 us (0.966)
  waiting for transfers between devices: 287 us -> 247 us
  blocking collectives: 0 us -> 29.7 us
    all_gather x1 -> x0, waiting for transfers between devices: 56.7 us -> none  [per_device(): lax.all_gather(first, 'con', axis=0, tiled=True)]
    all_to_all x0 -> x1, blocking collectives: none -> 29.7 us  [per_device(): lax.all_to_all(jnp.stack([first] * lax.axis_size('con')), 'con', 0, 0)]
    unnamed x6 -> x5, waiting for transfers between devices: 164 us -> 181 us
  transfers between devices with their start and end apart: 4 -> 3, of which waited for: 4 -> 3; matrix products, arithmetic and copies ran while one was open for 7% -> 7% of each run, Pallas kernels for 0% -> 0%
where the time goes in v1:
time: 344 us
  waiting for transfers between devices  247 us (72%)
  blocking collectives  29.7 us (9%)
  matrix products  24 us (7%)
  other arithmetic  15.3 us (4%)
  between operations  13.9 us (4%)
  local copies, waits for them, and re-layouts  13.6 us (4%)
    unnamed x5, waiting for transfers between devices  181 us
    all_gather x1, waiting for transfers between devices, per_device(): lax.all_gather(own, 'res', axis=0, tiled=True)  65.8 us
    all_to_all x1, blocking collectives, per_device(): lax.all_to_all(jnp.stack([first] * lax.axis_size('con')), 'con', 0, 0)  29.7 us
    unnamed x2, matrix products  20.7 us
    mul x1, other arithmetic, per_device(): integrals.reshape(tiles_down, W, tiles_across, W)  12.2 us
    unnamed x15, local copies, waits for them, and re-layouts  10.9 us
  transfers between devices with their start and end apart: 3, of which 3 were waited for; matrix products, arithmetic and copies ran while one was open for 7% of the time, Pallas kernels for 0%

profile of v1, /device:TPU:4, one launch (start us, length us, event | category | flops | bytes accessed | tf_op | source)
XLA Modules:
  0.0 343.6 jit_solution(12973362117167730066)
XLA Ops:
  7.2 0.7 broadcast_select_fusion
  7.9 0.7 iota_minimum_fusion
  8.6 0.2 convert_reduce_fusion
  8.9 0.4 convolution_bitcast_fusion.1
  9.3 0.7 copy.20
  10.1 0.7 convert_element_type.5
  10.8 0.9 mul.69
  11.7 8.4 %copy.30 = f32[192,8,6,256]{3,1,2,0:T(8,128)} copy(f32[192,8,6,256]{3,2,1,0:T(8,128)S(1)} %bitcast.37) | data formatting | bytes 18874368
  20.0 12.2 %mul.71 = f32[1536,1536]{1,0:T(8,128)} multiply(f32[1536,1536]{1,0:T(8,128)} %param.10, f32[1536,1536]{1,0:T(8,128)} %bitcast.38) | non-fusion elementwise | flops 2359296 | bytes 28311552 | tf_op jit(solution)/shard_map/mul | solution.py:47
  32.3 65.8 %all-gather.2.cloned.1.call-done = f32[1536,192]{1,0:T(8,128)} async-done(((f32[96,192]{1,0:T(8,128)}), f32[1536,192]{1,0:T(8,128)}) %all-gather.2.cloned.1.call-update) | async-done | bytes 1179664 | tf_op jit(solution)/shard_map/all_gather | solution.py:77
  98.1 9.3 %fusion.30 = f32[1536,192]{1,0:T(8,128)} fusion(f32[1536,1536]{1,0:T(8,128)} %mul.71, f32[1536,192]{1,0:T(8,128)} %all-gather.2.cloned.1.call-done), kind=kOutput, calls=%fused_computation.63 | convolution fusion | flops 2717908992 | bytes 11796480
  107.5 0.6 copy-done.2
  108.2 0.8 constant_dynamic-slice_fusion.1
  109.0 0.5 select_reduce_fusion
  109.6 78.8 %reduce-scatter.7.cloned.1.call-done = f32[96,192]{1,0:T(8,128)} async-done(((f32[1536,192]{1,0:T(8,128)}), f32[96,192]{1,0:T(8,128)}) %reduce-scatter.7.cloned.1.call-update) | async-done | bytes 73744
  188.4 1.0 copy.27
  189.4 0.4 fusion.3
  190.1 29.7 %all_to_all.5 = f32[16,96,192]{2,1,0:T(8,128)S(1)} all-to-all(f32[16,96,192]{2,1,0:T(8,128)S(1)} %stack.2), channel_id=1, replica_groups=mesh['con'=16,'res'=16] {'con'}, dimensions={0} | all-to-all | bytes 2359296 | tf_op jit(solution)/shard_map/all_to_all | solution.py:88
  219.8 11.3 %fusion.31 = f32[1536,192]{1,0:T(8,128)} fusion(f32[1536,1536]{1,0:T(8,128)} %mul.71, f32[1536,192]{1,0:T(8,128)S(1)} %bitcast.39), kind=kOutput, calls=%fused_computation.64 | convolution fusion | flops 2717908992 | bytes 11796480
  231.2 1.1 convolution_multiply_fusion.1
  232.2 102.3 %reduce-scatter.9.cloned.1.call-done = f32[96,192]{1,0:T(8,128)} async-done(((f32[1536,192]{1,0:T(8,128)}), f32[96,192]{1,0:T(8,128)}) %reduce-scatter.9.cloned.1.call-update) | async-done | bytes 73744
  334.6 1.0 copy.29
  335.6 0.4 fusion.1
  336.0 1.1 convolution_multiply_fusion
  (26 shorter events, 0.7 us)
Async XLA Ops:
  7.2 1.7 copy-start
  7.2 90.9 %all-gather.2.cloned.1.call-start = ((), (), s32[]{:S(2)}) async-start(), calls=%async_computation.3 | async-start | bytes 1671168 | tf_op jit(solution)/shard_map/all_gather | solution.py:77
  10.0 178.4 %reduce-scatter.7.cloned.1.call-start = ((), (), s32[]{:S(2)}) async-start(), calls=%async_computation.4 | async-start | bytes 1671168
  107.4 0.7 copy-start.2
  107.4 0.7 copy-start.3
  107.4 1.6 copy-start.1
  107.4 82.0 %copy-start.4 = (f32[96,384]{1,0:T(8,128)S(1)}, f32[96,384]{1,0:T(8,128)}, u32[]{:S(2)}) copy-start(f32[96,384]{1,0:T(8,128)} %param.13) | copy-start | bytes 442372
  107.4 227.2 %reduce-scatter.9.cloned.1.call-start = ((), (), s32[]{:S(2)}) async-start(), calls=%async_computation.5 | async-start | bytes 1671168
  231.1 104.4 %copy-start.5 = (f32[96,384]{1,0:T(8,128)S(1)}, f32[96,384]{1,0:T(8,128)}, u32[]{:S(2)}) copy-start(f32[96,384]{1,0:T(8,128)} %param.14) | copy-start | bytes 442372
Sparse Core Ops, SparseCore 0:
  10.4 87.6 all-gather.1
  107.5 80.8 reduce-scatter.6
  231.3 103.2 reduce-scatter.8
